TPU v7x, 32 devices: a whole 2x2x4 slice. The times are simulated.
32 devices in a mesh: expert: 4 (over y, x), fsdp: 8 (over z, core).
Axes of the slice: x: 2, y: 2, z: 4, core: 2. Of those that a mesh axis runs over, the one named last changes fastest.
Arguments:
- tokens: bfloat16 [4608, 2048], P(('expert', 'fsdp')), may hold values from -6 to 6
- expert_ids: int32 [4608, 6], P(('expert', 'fsdp')), may hold values from 0 to 15, as said below
- combine: float32 [4608, 6], P(('expert', 'fsdp')), may hold values from 0.05 to 1
- gate_weight: bfloat16 [16, 1408, 2048], P('expert', 'fsdp'), may hold values from -0.125 to 0.125
- up_weight: bfloat16 [16, 1408, 2048], P('expert', 'fsdp'), may hold values from -0.125 to 0.125
- down_weight: bfloat16 [16, 1408, 2048], P('expert', 'fsdp'), may hold values from -0.15625 to 0.15625
Outputs:
- mixed: bfloat16 [4608, 2048], P(('expert', 'fsdp'))
Inputs may be any that keep to these rules, and one draw needn't show every extreme that they name: `expert_ids`: each row names 6 different experts. Within the 144 rows of each device no expert is named more than 72 times, and one and the same expert is named exactly 72 times by the rows of every device.
All inputs are finite; a program needn't handle non-finite values.
Results may differ from a plain program's by a relative error of at most 0.0058.
Values may be sent and summed in bfloat16 or wider, within the bound.
No kernel may reach another device: no remote copies, remote signals or barrier semaphores. Data moves between devices by JAX's collectives and lax.ppermute only.
A program may use at most 128 MiB of HBM per device.

v0:
```python
import jax
import jax.numpy as jnp
from jax import lax
from jax.sharding import PartitionSpec as P

CAP = 72


def add_piece(expert_rows, pieces):
    gate_piece, up_piece, down_piece = pieces
    gate_pre = jnp.einsum(
        "grd,gfd->grf", expert_rows, gate_piece, preferred_element_type=jnp.float32
    )
    up_pre = jnp.einsum("grd,gfd->grf", expert_rows, up_piece, preferred_element_type=jnp.float32)
    hidden = (jax.nn.silu(gate_pre) * up_pre).astype(jnp.bfloat16)
    return jnp.einsum("grf,gfd->grd", hidden, down_piece, preferred_element_type=jnp.float32)


def per_device(tokens, expert_ids, combine, gate_weight, up_weight, down_weight):
    groups = lax.axis_size("expert")
    per_group = gate_weight.shape[0]
    tok_rows, top_k = expert_ids.shape
    model_width = tokens.shape[1]
    flat_ids = expert_ids.reshape(-1)
    onehot = (flat_ids[:, None] == jnp.arange(per_group * groups, dtype=jnp.int32)[None, :]).astype(
        jnp.int32
    )
    earlier = jnp.cumsum(onehot, axis=0) - onehot
    rank_within = jnp.sum(earlier * onehot, axis=1)
    owner_group = flat_ids // per_group
    within = flat_ids % per_group
    slot_index = (within * groups + owner_group) * CAP + rank_within
    source = jnp.arange(tok_rows * top_k, dtype=jnp.int32) // top_k
    outgoing = (
        jnp.zeros((per_group * groups * CAP, model_width), jnp.bfloat16)
        .at[slot_index]
        .set(tokens[source])
    )
    outgoing = outgoing.reshape(per_group, groups, CAP, model_width)
    arrived = lax.all_to_all(outgoing, "expert", split_axis=1, concat_axis=1, tiled=True)
    expert_rows = arrived.reshape(per_group, groups * CAP, model_width)
    summed = add_piece(
        expert_rows,
        (
            lax.all_gather(gate_weight, "fsdp", axis=1, tiled=True),
            lax.all_gather(up_weight, "fsdp", axis=1, tiled=True),
            lax.all_gather(down_weight, "fsdp", axis=1, tiled=True),
        ),
    )
    produced = summed.astype(jnp.bfloat16)
    produced = produced.reshape(per_group, groups, CAP, model_width)
    returned = lax.all_to_all(produced, "expert", split_axis=1, concat_axis=1, tiled=True)
    back_rows = returned.reshape(per_group * groups * CAP, model_width)[slot_index]
    weighted = (
        back_rows.astype(jnp.float32).reshape(tok_rows, top_k, model_width) * combine[:, :, None]
    )
    return jnp.sum(weighted, axis=1).astype(jnp.bfloat16)


def solution(mesh):
    return jax.shard_map(
        per_device,
        mesh=mesh,
        in_specs=(
            P(("expert", "fsdp"), None),
            P(("expert", "fsdp"), None),
            P(("expert", "fsdp"), None),
            P("expert", "fsdp", None),
            P("expert", "fsdp", None),
            P("expert", "fsdp", None),
        ),
        out_specs=P(("expert", "fsdp"), None),
        check_vma=False,
    )
```

profile of v0, /device:TPU:0, one launch (start us, length us, event | category | flops | bytes accessed | tf_op | source)
XLA Modules:
  0.0 746.7 jit_solution(11843986732375107055)
XLA Ops:
  6.5 0.0 copy-start
  6.5 0.0 copy-start.2
  6.5 0.0 all-gather.4.cloned.1.call-start
  6.5 0.7 all-gather.4.cloned.1.call-update
  7.3 0.0 all-gather.6.cloned.1.call-start
  7.3 0.7 all-gather.6.cloned.1.call-update
  8.0 0.0 all-gather.8.cloned.1.call-start
  8.1 0.7 all-gather.8.cloned.1.call-update
  8.7 0.0 copy-done.2
  8.8 0.1 copy.21
  8.9 0.1 eq.24
  9.0 0.1 reshape.195
  9.2 2.0 reduce-window.6
  11.2 0.3 slice_reduce_fusion
  11.5 0.1 bitcast_bitcast_fusion
  11.7 0.0 copy-done
  11.7 23.2 %scatter_custom_fusion = bf16[1152,2048]{1,0:T(8,128)(2,1)} fusion(s32[864]{0:T(1024)S(1)} %fusion.5, bf16[144,2048]{1,0:T(8,128)(2,1)S(1)} %copy-done, s32[1024]{0:T(1024)S(1)} %pad_clamp_fusion.1, bf16[]{:T(256)} %constant.42.clone.1), kind=kCustom, calls=%fused_computation.6 | custom fusion | bytes 4718594 | tf_op jit(solution)/shard_map/scatter | solution.py:37
  34.9 2.8 copy.25
  37.7 58.4 %all_to_all.10 = bf16[4,4,72,2048]{3,2,0,1:T(8,128)(2,1)S(1)} all-to-all(bf16[4,4,72,2048]{3,2,0,1:T(8,128)(2,1)S(1)} %copy.25), channel_id=1, replica_groups=mesh['expert'=4,'fsdp'=8] {'expert'}, dimensions={1} | all-to-all | bytes 9437184 | tf_op jit(solution)/shard_map/all_to_all | solution.py:40
  96.1 2.6 copy.26
  98.7 115.7 %all-gather.4.cloned.1.call-done = bf16[4,1408,2048]{2,1,0:T(8,128)(2,1)} async-done(((bf16[4,176,2048]{2,1,0:T(8,128)(2,1)}), bf16[4,1408,2048]{2,1,0:T(8,128)(2,1)}) %all-gather.4.cloned.1.call-update) | async-done | bytes 23068688 | tf_op jit(solution)/shard_map/all_gather | solution.py:45
  214.4 16.9 %fusion.9 = f32[4,288,1408]{2,1,0:T(8,128)} fusion(bf16[4,288,2048]{2,1,0:T(8,128)(2,1)} %bitcast.33, bf16[4,1408,2048]{2,1,0:T(8,128)(2,1)} %all-gather.4.cloned.1.call-done), kind=kOutput, calls=%fused_computation.36 | convolution fusion | flops 6643777536 | bytes 34275328 | tf_op jit(solution)/shard_map/grd,gfd->grf/dot_general | solution.py:11
  231.3 185.6 %all-gather.6.cloned.1.call-done = bf16[4,1408,2048]{2,1,0:T(8,128)(2,1)} async-done(((bf16[4,176,2048]{2,1,0:T(8,128)(2,1)}), bf16[4,1408,2048]{2,1,0:T(8,128)(2,1)}) %all-gather.6.cloned.1.call-update) | async-done | bytes 23068688 | tf_op jit(solution)/shard_map/all_gather | solution.py:46
  416.9 202.5 %all-gather.8.cloned.1.call-done = bf16[4,1408,2048]{2,1,0:T(8,128)(2,1)} async-done(((bf16[4,176,2048]{2,1,0:T(8,128)(2,1)}), bf16[4,1408,2048]{2,1,0:T(8,128)(2,1)}) %all-gather.8.cloned.1.call-update) | async-done | bytes 23068688 | tf_op jit(solution)/shard_map/all_gather | solution.py:47
  619.4 24.4 %convolution_convert_fusion = bf16[4,288,2048]{2,1,0:T(8,128)(2,1)} fusion(bf16[4,1408,2048]{2,1,0:T(8,128)(2,1)} %all-gather.8.cloned.1.call-done, f32[4,288,1408]{2,1,0:T(8,128)} %fusion.9, bf16[4,288,2048]{2,1,0:T(8,128)(2,1)} %bitcast.34, bf16[4,1408,2048]{2,1,0:T(8,128)(2,1)} %all-gather.6.cloned.1.call-done), kind=kOutput, calls=%fused_computation.5 | convolution fusion | flops 13299646464 | bytes 62062592 | tf_op jit(solution)/shard_map/grf,gfd->grd/dot_general | solution.py:16
  643.8 5.2 copy.27
  649.0 0.0 copy-start.3
  649.0 5.3 all-to-all-start.1
  654.3 0.0 copy-done.3
  654.3 0.1 copy.29
  654.4 53.4 %all-to-all-done.1 = bf16[4,4,72,2048]{3,2,0,1:T(8,128)(2,1)} async-done(((bf16[4,4,72,2048]{3,2,0,1:T(8,128)(2,1)}), bf16[4,4,72,2048]{3,2,0,1:T(8,128)(2,1)}, u32[]{:S(2)}, u32[]{:S(2)}) %all-to-all-start.1) | async-done | bytes 4718624 | tf_op jit(solution)/shard_map/all_to_all | solution.py:52
  707.8 5.2 copy.28
  713.0 11.7 %gather_fusion = bf16[864,2048]{1,0:T(8,128)(2,1)} fusion(bf16[1152,2048]{1,0:T(8,128)(2,1)} %bitcast.31, s32[1024]{0:T(1024)S(1)} %pad_clamp_fusion), kind=kCustom, calls=%fused_computation.1 | custom fusion | bytes 7081344 | tf_op jit(solution)/shard_map/gather | solution.py:53
  724.7 0.0 copy-start.1
  724.7 7.2 reshape.203
  731.9 8.2 %multiply_reduce_fusion = bf16[144,2048]{1,0:T(8,128)(2,1)} fusion(f32[144,6,2048]{2,1,0:T(8,128)} %reshape.203, f32[144,6]{1,0:T(8,128)S(1)} %copy.29), kind=kLoop, calls=%fused_computation.3 | loop fusion | flops 3244032 | bytes 7671168 | tf_op jit(solution)/shard_map/reduce_sum | solution.py:57
  740.1 0.0 copy-done.1
  (8 shorter events, 0.2 us)
Async XLA Ops:
  6.5 5.2 copy-start
  6.5 2.2 copy-start.2
  6.5 207.8 %all-gather.4.cloned.1.call-start = ((), (), s32[]{:S(2)}) async-start(), calls=%async_computation.2 | async-start | bytes 25952256 | tf_op jit(solution)/shard_map/all_gather | solution.py:45
  7.3 409.6 %all-gather.6.cloned.1.call-start = ((), (), s32[]{:S(2)}) async-start(), calls=%async_computation.3 | async-start | bytes 25952256 | tf_op jit(solution)/shard_map/all_gather | solution.py:46
  8.0 611.4 %all-gather.8.cloned.1.call-start = ((), (), s32[]{:S(2)}) async-start(), calls=%async_computation.4 | async-start | bytes 25952256 | tf_op jit(solution)/shard_map/all_gather | solution.py:47
  649.0 5.3 copy-start.3
  649.0 58.8 %all-to-all-start.1 = ((bf16[4,4,72,2048]{3,2,0,1:T(8,128)(2,1)}), bf16[4,4,72,2048]{3,2,0,1:T(8,128)(2,1)}, u32[]{:S(2)}, u32[]{:S(2)}) async-start(bf16[4,4,72,2048]{3,2,0,1:T(8,128)(2,1)} %copy.27), calls=%async_computation.1 | async-start | bytes 9437184 | tf_op jit(solution)/shard_map/all_to_all | solution.py:52
  724.7 15.4 %copy-start.1 = (bf16[144,2048]{1,0:T(8,128)(2,1)S(1)}, bf16[144,2048]{1,0:T(8,128)(2,1)}, u32[]{:S(2)}) copy-start(bf16[144,2048]{1,0:T(8,128)(2,1)} %param.6) | copy-start | bytes 1769476
Sparse Core Ops, SparseCore 0:
  9.0 205.3 all-gather.3
  216.0 200.8 all-gather.5
  418.5 200.8 all-gather.7
where the time goes:
time: 747 us
  waiting for transfers between devices  559 us (75%)
  local copies, waits for them, and re-layouts  58.7 us (8%)
  blocking collectives  58.4 us (8%)
  matrix products  41.3 us (6%)
  between operations  13.2 us (2%)
  other arithmetic  10.4 us (1%)
    all_gather x1, waiting for transfers between devices, per_device(): lax.all_gather(down_weight, 'fsdp', axis=1, tiled=True)  203 us
    all_gather x1, waiting for transfers between devices, per_device(): lax.all_gather(up_weight, 'fsdp', axis=1, tiled=True)  186 us
    all_gather x1, waiting for transfers between devices, per_device(): lax.all_gather(gate_weight, 'fsdp', axis=1, tiled=True)  116 us
    all_to_all x1, blocking collectives, per_device(): lax.all_to_all(outgoing, 'expert', split_axis=1, concat_axis=1, tiled=True)  58.4 us
    all_to_all x1, waiting for transfers between devices, per_device(): lax.all_to_all(produced, 'expert', split_axis=1, concat_axis=1, tiled=True)  53.4 us
    dot_general x1, matrix products, add_piece(): jnp.einsum('grf,gfd->grd', hidden, down_piece, preferred_element_type=jnp...  24.4 us
    scatter x1, local copies, waits for them, and re-layouts, per_device(): outgoing = jnp.zeros((per_group * groups * CAP, model_width), jnp.bfloat1...  23.2 us
    dot_general x1, matrix products, add_piece(): jnp.einsum('grd,gfd->grf', expert_rows, gate_piece, preferred_element_typ...  16.9 us
  transfers between devices with their start and end apart: 4, of which 4 were waited for; matrix products, arithmetic and copies ran while one was open for 6% of the time, Pallas kernels for 0%

commit v1 on v0

v1 whole, which is shorter than its diff:
```python
import jax
import jax.numpy as jnp
from jax import lax
from jax.sharding import Mesh, PartitionSpec as P

PLANE = ("e_hi", "e_lo", "line")
AXES = ("e_hi", "e_lo", "line", "core")


def half_hidden(rows, col_weight, gate, up):
    gate_pre = lax.dot_general(
        rows, gate, (((1,), (1,)), ((), ())), preferred_element_type=jnp.float32
    )
    up_pre = lax.dot_general(
        rows, up, (((1,), (1,)), ((), ())), preferred_element_type=jnp.float32
    )
    return (jax.nn.silu(gate_pre) * up_pre * col_weight).astype(jnp.bfloat16)


def per_device(tokens, expert_ids, combine, gate_weight, up_weight, down_weight):
    groups = lax.axis_size("e_hi") * lax.axis_size("e_lo")
    group = lax.axis_index(("e_hi", "e_lo"))
    per_group, units, width = gate_weight.shape
    experts = groups * per_group
    chosen = expert_ids[:, :, None] == jnp.arange(experts, dtype=jnp.int32)[None, None, :]
    dense_weight = jnp.sum(jnp.where(chosen, combine[:, :, None], 0.0), axis=1)

    swap = [(0, 1), (1, 0)]
    flat = [w.reshape(per_group * units, width) for w in (gate_weight, up_weight, down_weight)]
    other = [lax.ppermute(w, "core", swap) for w in flat]

    all_weight = lax.all_gather(dense_weight, PLANE, axis=0, tiled=True)
    rows = lax.all_gather(tokens, PLANE, axis=0, tiled=True)
    mine = lax.dynamic_slice_in_dim(all_weight, group * per_group, per_group, axis=1)
    column = jnp.arange(per_group * units, dtype=jnp.int32)[None, :]
    col_weight = mine[:, per_group - 1 :]
    for i in range(per_group - 2, -1, -1):
        col_weight = jnp.where(column < (i + 1) * units, mine[:, i : i + 1], col_weight)
    hidden = [half_hidden(rows, col_weight, gate, up) for gate, up, _ in (flat, other)]
    down = jnp.concatenate([flat[2], other[2]], axis=0)
    partial = jnp.dot(
        jnp.concatenate(hidden, axis=1), down, preferred_element_type=jnp.float32
    ).astype(jnp.bfloat16)
    return lax.psum_scatter(partial, PLANE, scatter_dimension=0, tiled=True)


def solution(mesh):
    groups, shards = mesh.shape["expert"], mesh.shape["fsdp"]
    split = Mesh(mesh.devices.reshape(groups // 2, 2, shards // 2, 2), AXES)
    whole, expert, shard = P(AXES, None), ("e_hi", "e_lo"), ("line", "core")
    return jax.shard_map(
        per_device,
        mesh=split,
        in_specs=(whole, whole, whole) + (P(expert, shard, None),) * 3,
        out_specs=whole,
        check_vma=False,
    )
```

time: 747 us -> 370 us (0.50)
  waiting for transfers between devices: 559 us -> 251 us
  local copies, waits for them, and re-layouts: 58.7 us -> 0.45 us
  matrix products: 41.3 us -> 56.8 us
  blocking collectives: 58.4 us -> 46.4 us
  other arithmetic: 10.4 us -> 0.75 us
    all_gather x3 -> x1, waiting for transfers between devices: 504 us -> 81.8 us  [per_device(): rows = lax.all_gather(tokens, PLANE, axis=0, tiled=True)]
    reduce_scatter x0 -> x1, waiting for transfers between devices: none -> 168 us  [per_device(): return lax.psum_scatter(partial, PLANE, scatter_dimension=0, tiled=True)]
    all_to_all x1 -> x0, blocking collectives: 58.4 us -> none  [per_device(): lax.all_to_all(outgoing, 'expert', split_axis=1, concat_axis=1, tiled=True)]
    all_to_all x1 -> x0, waiting for transfers between devices: 53.4 us -> none  [per_device(): lax.all_to_all(produced, 'expert', split_axis=1, concat_axis=1, tiled=True)]
    all_gather x0 -> x1, blocking collectives: none -> 46.4 us  [per_device(): all_weight = lax.all_gather(dense_weight, PLANE, axis=0, tiled=True)]
    scatter x1 -> x0, local copies, waits for them, and re-layouts: 23.2 us -> none  [per_device(): outgoing = jnp.zeros((per_group * groups * CAP, model_width), jnp.bfloat1...]
    dot_general x2 -> x5, matrix products: 41.3 us -> 56.8 us  [the longest x1 19 us: per_device(): jnp.dot(jnp.concatenate(hidden, axis=1), down, preferred_element_type=jnp...]
    gather x1 -> x0, local copies, waits for them, and re-layouts: 11.7 us -> none  [per_device(): returned.reshape(per_group * groups * CAP, model_width)[slot_index]]
  transfers between devices with their start and end apart: 4 -> 5, of which waited for: 4 -> 2; matrix products, arithmetic and copies ran while one was open for 6% -> 11% of each run, Pallas kernels for 0% -> 0%
where the time goes in v1:
time: 370 us
  waiting for transfers between devices  251 us (68%)
  matrix products  56.8 us (15%)
  blocking collectives  46.4 us (13%)
  between operations  13.5 us (4%)
    reduce_scatter x1, waiting for transfers between devices, per_device(): return lax.psum_scatter(partial, PLANE, scatter_dimension=0, tiled=True)  168 us
    all_gather x1, waiting for transfers between devices, per_device(): rows = lax.all_gather(tokens, PLANE, axis=0, tiled=True)  81.8 us
    all_gather x1, blocking collectives, per_device(): all_weight = lax.all_gather(dense_weight, PLANE, axis=0, tiled=True)  46.4 us
    dot_general x1, matrix products, per_device(): jnp.dot(jnp.concatenate(hidden, axis=1), down, preferred_element_type=jnp...  19 us
    dot_general x2, matrix products, half_hidden(): lax.dot_general(rows, gate, (((1,), (1,)), ((), ())), preferred_element_t...  19 us
    dot_general x2, matrix products, half_hidden(): lax.dot_general(rows, up, (((1,), (1,)), ((), ())), preferred_element_typ...  18.8 us
  transfers between devices with their start and end apart: 5, of which 2 were waited for; matrix products, arithmetic and copies ran while one was open for 11% of the time, Pallas kernels for 0%

profile of v1, /device:TPU:0, one launch (start us, length us, event | category | flops | bytes accessed | tf_op | source)
XLA Modules:
  0.0 370.0 jit_solution(6103369238086779629)
XLA Ops:
  6.5 0.0 all-gather.3.cloned.1.call-start
  6.5 0.7 all-gather.3.cloned.1.call-update
  7.3 0.0 reduce-scatter.2.cloned.1.call-start
  7.3 0.5 collective-permute-start
  7.8 0.1 collective-permute-start.1
  7.9 0.4 collective-permute-start.2
  8.3 0.7 select_reduce_fusion
  9.1 46.4 %all-gather = f32[16,144,16]{1,2,0:T(8,128)S(1)} all-gather(f32[1,144,16]{1,2,0:T(8,128)S(1)} %bitcast.14), channel_id=1, replica_groups=mesh['e_hi'=2,'e_lo'=2,'line'=4,'core'=2] {'e_hi','e_lo','line'}, dimensions={0}, use_global_device_ids=true | all-gather | bytes 156672 | tf_op jit(solution)/shard_map/all_gather | solution.py:32
  55.5 0.2 copy.16
  55.6 0.2 reshape.30
  55.8 0.1 dynamic-slice_reduce_fusion.3
  55.9 0.0 copy-start.1
  55.9 81.8 %all-gather.3.cloned.1.call-done = bf16[2304,2048]{1,0:T(8,128)(2,1)} async-done(((bf16[144,2048]{1,0:T(8,128)(2,1)}), bf16[2304,2048]{1,0:T(8,128)(2,1)}) %all-gather.3.cloned.1.call-update) | async-done | bytes 9437200 | tf_op jit(solution)/shard_map/all_gather | solution.py:33
  137.7 0.0 copy-start
  137.7 10.3 %fusion.7 = f32[2304,704]{0,1:T(8,128)S(1)} fusion(bf16[2304,2048]{1,0:T(8,128)(2,1)} %all-gather.3.cloned.1.call-done, bf16[704,2048]{1,0:T(8,128)(2,1)} %bitcast.16), kind=kOutput, calls=%fused_computation.20 | convolution fusion | flops 6643777536 | bytes 18808832 | tf_op jit(solution)/shard_map/dot_general | solution.py:11
  148.0 0.0 copy-done.1
  148.0 0.0 copy-done
  148.0 8.5 %multiply_convert_fusion.1 = bf16[2304,704]{0,1:T(8,128)(2,1)S(1)} fusion(f32[2304,704]{0,1:T(8,128)S(1)} %fusion.7, bf16[2304,2048]{1,0:T(8,128)(2,1)S(1)} %copy-done, bf16[704,2048]{1,0:T(8,128)(2,1)S(1)} %bitcast.18, f32[2304]{0:T(1024)S(1)} %get-tuple-element.8, f32[2304]{0:T(1024)S(1)} %get-tuple-element.6, f32[2304]{0:T(1024)S(1)} %get-tuple-element.7, ...), kind=kOutput, calls=%fused_computation.5 | convolution fusion | flops 6659997696 | bytes 22091840 | tf_op jit(solution)/shard_map/dot_general | solution.py:14
  156.6 0.0 collective-permute-done
  156.6 8.7 %fusion.8 = f32[2304,704]{0,1:T(8,128)S(1)} fusion(bf16[2304,2048]{1,0:T(8,128)(2,1)S(1)} %copy-done, bf16[704,2048]{1,0:T(8,128)(2,1)} %collective-permute-done), kind=kOutput, calls=%fused_computation.21 | convolution fusion | flops 6643777536 | bytes 18808832 | tf_op jit(solution)/shard_map/dot_general | solution.py:11
  165.3 0.0 copy-start.2
  165.3 0.0 collective-permute-done.1
  165.3 10.3 %multiply_convert_fusion = bf16[2304,704]{0,1:T(8,128)(2,1)S(1)} fusion(f32[2304,704]{0,1:T(8,128)S(1)} %fusion.8, f32[2304]{0:T(1024)S(1)} %get-tuple-element.8, f32[2304]{0:T(1024)S(1)} %get-tuple-element.6, f32[2304]{0:T(1024)S(1)} %get-tuple-element.7, f32[2304]{0:T(1024)S(1)} %get-tuple-element.5, pred[704]{0:T(1024)(128)(4,1)S(1)} %get-tuple-element.9, ...), kind=kOutput, calls=%fused_computation.4 | convolution fusion | flops 6659997696 | bytes 22091840 | tf_op jit(solution)/shard_map/dot_general | solution.py:14
  175.6 0.0 collective-permute-done.2
  175.6 0.0 copy-done.2
  175.6 19.0 %convolution_convert_fusion = bf16[2304,2048]{1,0:T(8,128)(2,1)} fusion(bf16[2304,704]{0,1:T(8,128)(2,1)S(1)} %multiply_convert_fusion, bf16[2304,704]{0,1:T(8,128)(2,1)S(1)} %multiply_convert_fusion.1, bf16[704,2048]{1,0:T(8,128)(2,1)} %collective-permute-done.2, bf16[704,2048]{1,0:T(8,128)(2,1)S(1)} %bitcast.20), kind=kOutput, calls=%fused_computation | convolution fusion | flops 13316784128 | bytes 21692416 | tf_op jit(solution)/shard_map/dot_general | solution.py:41
  194.6 0.0 reduce-scatter.2.cloned.1.call-update
  194.7 168.5 %reduce-scatter.2.cloned.1.call-done = bf16[144,2048]{1,0:T(8,128)(2,1)} async-done(((bf16[2304,2048]{1,0:T(8,128)(2,1)}), bf16[144,2048]{1,0:T(8,128)(2,1)}) %reduce-scatter.2.cloned.1.call-update) | async-done | bytes 589840 | tf_op jit(solution)/shard_map/reduce_scatter | solution.py:44
  (2 shorter events, 0.0 us)
Async XLA Ops:
  6.5 131.2 %all-gather.3.cloned.1.call-start = ((), (), s32[]{:S(2)}) async-start(), calls=%async_computation.1 | async-start | bytes 10027008 | tf_op jit(solution)/shard_map/all_gather | solution.py:33
  7.3 355.9 %reduce-scatter.2.cloned.1.call-start = ((), (), s32[]{:S(2)}) async-start(), calls=%async_computation.2 | async-start | bytes 10027008 | tf_op jit(solution)/shard_map/reduce_scatter | solution.py:44
  7.3 149.3 %collective-permute-start = (bf16[704,2048]{1,0:T(8,128)(2,1)}, bf16[704,2048]{1,0:T(8,128)(2,1)}, u32[]{:S(2)}, u32[]{:S(2)}) collective-permute-start(bf16[704,2048]{1,0:T(8,128)(2,1)} %bitcast.15), channel_id=1, source_target_pairs={{0,1},{1,0},{2,3},{3,2},{4,5},{5,4},{6,7},{7,6},{8,9},{9,8},{10,11... | collective-permute-start | bytes 8650760 | tf_op jit(solution)/shard_map/ppermute | solution.py:30
  7.8 157.5 %collective-permute-start.1 = (bf16[704,2048]{1,0:T(8,128)(2,1)}, bf16[704,2048]{1,0:T(8,128)(2,1)}, u32[]{:S(2)}, u32[]{:S(2)}) collective-permute-start(bf16[704,2048]{1,0:T(8,128)(2,1)} %bitcast.17), channel_id=1, source_target_pairs={{0,1},{1,0},{2,3},{3,2},{4,5},{5,4},{6,7},{7,6},{8,9},{9,8},{10,11... | collective-permute-start | bytes 8650760 | tf_op jit(solution)/shard_map/ppermute | solution.py:30
  7.9 167.7 %collective-permute-start.2 = (bf16[704,2048]{1,0:T(8,128)(2,1)}, bf16[704,2048]{1,0:T(8,128)(2,1)}, u32[]{:S(2)}, u32[]{:S(2)}) collective-permute-start(bf16[704,2048]{1,0:T(8,128)(2,1)} %bitcast.19), channel_id=1, source_target_pairs={{0,1},{1,0},{2,3},{3,2},{4,5},{5,4},{6,7},{7,6},{8,9},{9,8},{10,11... | collective-permute-start | bytes 8650760 | tf_op jit(solution)/shard_map/ppermute | solution.py:30
  55.9 92.1 %copy-start.1 = (bf16[4,176,2048]{2,1,0:T(8,128)(2,1)S(1)}, bf16[4,176,2048]{2,1,0:T(8,128)(2,1)}, u32[]{:S(2)}) copy-start(bf16[4,176,2048]{2,1,0:T(8,128)(2,1)} %param.10) | copy-start | bytes 8650756
  137.7 10.3 %copy-start = (bf16[2304,2048]{1,0:T(8,128)(2,1)S(1)}, bf16[2304,2048]{1,0:T(8,128)(2,1)}, u32[]{:S(2)}) copy-start(bf16[2304,2048]{1,0:T(8,128)(2,1)} %all-gather.3.cloned.1.call-done) | copy-start | bytes 28311556
  165.3 10.3 %copy-start.2 = (bf16[4,176,2048]{2,1,0:T(8,128)(2,1)S(1)}, bf16[4,176,2048]{2,1,0:T(8,128)(2,1)}, u32[]{:S(2)}) copy-start(bf16[4,176,2048]{2,1,0:T(8,128)(2,1)} %param.11) | copy-start | bytes 8650756
Sparse Core Ops, SparseCore 0:
  10.1 127.5 all-gather.2
  194.8 168.2 reduce-scatter.1
